TPU v7x, 32 devices: a whole 2x2x4 slice. The times are simulated.
32 devices in a mesh: row: 8 (over y, x, core), col: 4 (over z).
Axes of the slice: x: 2, y: 2, z: 4, core: 2. Of those that a mesh axis runs over, the one named last changes fastest.
Arguments:
- u_factors: bfloat16 [24, 24, 1024, 128], P('row', 'col'), may hold values from -0.109375 to 0.109375
- v_factors: bfloat16 [24, 24, 1024, 128], P('row', 'col'), may hold values from -0.1875 to 0.1875
- tile_scales: float32 [24, 24, 128], P('row', 'col'), may hold values from 0.3 to 3
- rank_class: int32 [24, 24], P('row', 'col'), may hold values from 0 to 3, as said below
- slopes: float32 [64, 24576], P(None, 'row'), may hold values from -40 to 40
Outputs:
- solution_field: float32 [64, 24576], P(None, 'col')
- residual: float32 [64, 24576], P(None, 'col')
Inputs may be any that keep to these rules, and one draw needn't show every extreme that they name: `rank_class`: class k gives a tile of rank 128 / 8 * 2**k; tiles of one device tend to share high or low classes.
All inputs are finite; a program needn't handle non-finite values.
Results may differ from a plain program's by a relative error of at most 0.017.
Values may be sent and summed in bfloat16 or wider, within the bound.
A program may use at most 64 MiB of HBM per device.

v0:
```python
import jax
import jax.numpy as jnp
from jax import lax
from jax.sharding import PartitionSpec as P

ITERS = 2
damping = 0.1
epsilon = 1e-06


def rank_weights(tile_scales, rank_class):
    max_rank = tile_scales.shape[-1]
    ranks = jnp.left_shift(jnp.int32(max_rank // 8), rank_class)
    columns = lax.broadcasted_iota(jnp.int32, tile_scales.shape, 2)
    return jnp.where(columns < ranks[:, :, None], tile_scales, jnp.zeros_like(tile_scales))


def padded_apply(source, first_factor, second_factor, weights, transpose):
    rows_here, cols_here, tile_size, max_rank = first_factor.shape
    frames = source.shape[0]
    if transpose:
        pieces = source.reshape(frames, rows_here, tile_size)
        projected = jnp.einsum(
            "fis,ijsr->fijr", pieces, first_factor, preferred_element_type=jnp.float32
        )
        scaled = (projected * weights[None]).astype(jnp.bfloat16)
        result = jnp.einsum(
            "fijr,ijmr->fjm", scaled, second_factor, preferred_element_type=jnp.float32
        )
        return result.reshape(frames, cols_here * tile_size)
    pieces = source.reshape(frames, cols_here, tile_size)
    projected = jnp.einsum(
        "fjm,ijmr->fijr", pieces, first_factor, preferred_element_type=jnp.float32
    )
    scaled = (projected * weights[None]).astype(jnp.bfloat16)
    result = jnp.einsum("fijr,ijsr->fis", scaled, second_factor, preferred_element_type=jnp.float32)
    return result.reshape(frames, rows_here * tile_size)


def apply_tiles(source, first_factor, second_factor, weights, transpose):
    return padded_apply(source, first_factor, second_factor, weights, transpose)


def per_device(u_factors, v_factors, tile_scales, rank_class, slopes):
    weights = rank_weights(tile_scales, rank_class)
    rows_here, cols_here, tile_size, max_rank = u_factors.shape
    share_width = cols_here * tile_size // lax.axis_size("row")
    offset = lax.axis_index("row") * share_width

    def backward(image_b):
        partial_value = apply_tiles(image_b, u_factors, v_factors, weights, True)
        return lax.psum(partial_value, "row")

    def own_part(field):
        return lax.dynamic_slice_in_dim(field, offset, share_width, 1)

    def frame_product(left_field, right_field):
        return jnp.sum(own_part(left_field) * own_part(right_field), axis=1)

    right_side = backward(slopes.astype(jnp.bfloat16))
    solution_field = jnp.zeros_like(right_side)
    residual = right_side
    direction = right_side
    norm_now = lax.psum(frame_product(residual, residual), ("row", "col"))
    dir_norm = norm_now
    for sweep in range(ITERS):
        narrowed = direction.astype(jnp.bfloat16)
        forward_partial_value = apply_tiles(narrowed, v_factors, u_factors, weights, False)
        forward_image = lax.psum(forward_partial_value, "col")
        image_norm = lax.psum(jnp.sum(forward_image * forward_image, axis=1), "row")
        dir_norm = lax.psum(frame_product(direction, direction), ("row", "col"))
        operator_image = backward(forward_image.astype(jnp.bfloat16)) + damping * direction
        step_size = norm_now / (image_norm + damping * dir_norm + epsilon)
        solution_field = solution_field + step_size[:, None] * direction
        residual = residual - step_size[:, None] * operator_image
        if sweep + 1 < ITERS:
            norm_next = lax.psum(frame_product(residual, residual), ("row", "col"))
            growth = norm_next / (norm_now + epsilon)
            direction = residual + growth[:, None] * direction
            norm_now = norm_next
    return (solution_field, residual)


def solution(mesh):
    return jax.shard_map(
        per_device,
        mesh=mesh,
        in_specs=(
            P("row", "col", None, None),
            P("row", "col", None, None),
            P("row", "col", None),
            P("row", "col"),
            P(None, "row"),
        ),
        out_specs=(P(None, "col"), P(None, "col")),
        check_vma=False,
    )
```

profile of v0, /device:TPU:0, one launch (start us, length us, event | category | flops | bytes accessed | tf_op | source)
XLA Modules:
  0.0 383.3 jit_solution(15641545947727971645)
XLA Ops:
  10.4 6.1 %fusion.12 = f32[6,8,8,1024]{3,2,1,0:T(8,128)S(1)} fusion(bf16[3,6,1024,128]{3,2,1,0:T(8,128)(2,1)} %param.6, bf16[3,6,1024,128]{3,2,1,0:T(8,128)(2,1)} %param.5, bf16[64,3,1024,1]{2,1,0,3:T(4,128)(2,1)S(1)} %reshape.49, f32[3,6,128]{2,0,1:T(4,128)S(1)} %copy.12), kind=kOutput, calls=%fused_computation.16 | convolution fusion | flops 604274688 | bytes 11412480 | tf_op jit(solution)/shard_map/fijr,ijmr->fjm/dot_general | solution.py:27
  17.9 61.8 %all-reduce.6.cloned.1.call-done = f32[64,6144]{1,0:T(8,128)} async-done(((f32[64,6144]{1,0:T(8,128)}), f32[64,6144]{1,0:T(8,128)}) %all-reduce.6.cloned.1.call-update) | async-done | bytes 1572880 | tf_op jit(solution)/shard_map/psum | solution.py:52
  79.7 1.5 convert_element_type.42
  82.2 6.6 %convolution_bitcast_fusion.1 = f32[3,8,8,1024]{3,2,1,0:T(8,128)S(1)} fusion(bf16[3,6,1024,128]{3,2,1,0:T(8,128)(2,1)} %param.5, bf16[3,6,1024,128]{3,2,1,0:T(8,128)(2,1)} %param.6, bf16[64,6,1024,1]{2,1,0,3:T(8,128)(2,1)S(1)} %reshape.51, f32[3,6,128]{2,1,0:T(8,128)S(1)} %fusion.73), kind=kOutput, calls=%fused_computation.20 | convolution fusion | flops 604274688 | bytes 11019264 | tf_op jit(solution)/shard_map/fijr,ijsr->fis/dot_general | solution.py:36
  89.7 43.1 %all-reduce.8.cloned.1.call-done = f32[64,3072]{1,0:T(8,128)} async-done(((f32[64,3072]{1,0:T(8,128)}), f32[64,3072]{1,0:T(8,128)}) %all-reduce.8.cloned.1.call-update) | async-done | bytes 786448 | tf_op jit(solution)/shard_map/psum | solution.py:69
  132.9 1.6 multiply_reduce_fusion.1
  135.0 6.1 %fusion.15 = f32[6,8,8,1024]{3,2,1,0:T(8,128)S(1)} fusion(bf16[3,6,1024,128]{3,2,1,0:T(8,128)(2,1)} %param.6, bf16[3,6,1024,128]{3,2,1,0:T(8,128)(2,1)} %param.5, bf16[64,3,1024,1]{2,1,0,3:T(4,128)(2,1)S(1)} %reshape.53, f32[3,6,128]{2,0,1:T(4,128)S(1)} %copy.12), kind=kOutput, calls=%fused_computation.17 | convolution fusion | flops 604274688 | bytes 11412480 | tf_op jit(solution)/shard_map/fijr,ijmr->fjm/dot_general | solution.py:27
  143.9 39.8 %psum.74 = f32[64]{0:T(128)S(1)} all-reduce(f32[64]{0:T(128)S(1)} %multiply_reduce_fusion.4), channel_id=1, replica_groups=mesh['row'=8,'col'=4] {'row','col'}, use_global_device_ids=true, to_apply=%region_2.3 | all-reduce | flops 64 | bytes 512 | tf_op jit(solution)/shard_map/psum | solution.py:64
  183.8 12.9 %psum.76 = f32[64]{0:T(128)S(1)} all-reduce(f32[64]{0:T(128)S(1)} %get-tuple-element.8), channel_id=1, replica_groups=mesh['row'=8,'col'=4] {'row'}, use_global_device_ids=true, to_apply=%region_5.6 | all-reduce | flops 64 | bytes 512 | tf_op jit(solution)/shard_map/psum | solution.py:70
  196.7 4.7 %all-reduce.10.cloned.1.call-done = f32[64,6144]{1,0:T(8,128)} async-done(((f32[64,6144]{1,0:T(8,128)}), f32[64,6144]{1,0:T(8,128)}) %all-reduce.10.cloned.1.call-update) | async-done | bytes 1572880 | tf_op jit(solution)/shard_map/psum | solution.py:52
  201.4 1.7 multiply_subtract_fusion.1
  203.2 39.7 %psum.78 = f32[64]{0:T(128)S(1)} all-reduce(f32[64]{0:T(128)S(1)} %multiply_reduce_fusion.3), channel_id=1, replica_groups=mesh['row'=8,'col'=4] {'row','col'}, use_global_device_ids=true, to_apply=%region_8.9 | all-reduce | flops 64 | bytes 512 | tf_op jit(solution)/shard_map/psum | solution.py:77
  242.8 1.7 fusion.74
  244.5 2.8 reshape.55
  247.3 7.7 %convolution_bitcast_fusion = f32[3,8,8,1024]{3,2,1,0:T(8,128)} fusion(bf16[3,6,1024,128]{3,2,1,0:T(8,128)(2,1)} %param.5, bf16[3,6,1024,128]{3,2,1,0:T(8,128)(2,1)} %param.6, bf16[64,6,1024,1]{2,1,0,3:T(8,128)(2,1)} %reshape.55, f32[3,6,128]{2,1,0:T(8,128)S(1)} %fusion.73), kind=kOutput, calls=%fused_computation.19 | convolution fusion | flops 604274688 | bytes 11019264 | tf_op jit(solution)/shard_map/fijr,ijsr->fis/dot_general | solution.py:36
  255.1 2.1 copy.36
  257.2 43.6 %all-reduce.12.cloned.1.call-done = f32[64,3072]{1,0:T(8,128)} async-done(((f32[64,3072]{1,0:T(8,128)}), f32[64,3072]{1,0:T(8,128)}) %all-reduce.12.cloned.1.call-update) | async-done | bytes 786448 | tf_op jit(solution)/shard_map/psum | solution.py:69
  300.8 2.1 fusion.75
  304.1 7.4 %fusion.18 = f32[6,8,8,1024]{3,2,1,0:T(8,128)} fusion(bf16[3,6,1024,128]{3,2,1,0:T(8,128)(2,1)} %param.6, bf16[3,6,1024,128]{3,2,1,0:T(8,128)(2,1)} %param.5, bf16[64,3,1024,1]{2,1,0,3:T(4,128)(2,1)} %reshape.57, f32[3,6,128]{2,0,1:T(4,128)S(1)} %copy.12), kind=kOutput, calls=%fused_computation.18 | convolution fusion | flops 604274688 | bytes 11412480 | tf_op jit(solution)/shard_map/fijr,ijmr->fjm/dot_general | solution.py:27
  311.5 2.7 copy.37
  315.3 40.0 %psum.81 = f32[64]{0:T(128)S(1)} all-reduce(f32[64]{0:T(128)S(1)} %multiply_reduce_fusion.2), channel_id=1, replica_groups=mesh['row'=8,'col'=4] {'row','col'}, use_global_device_ids=true, to_apply=%region_13.14 | all-reduce | flops 64 | bytes 512 | tf_op jit(solution)/shard_map/psum | solution.py:71
  355.3 12.9 %psum.80 = f32[64]{0:T(128)S(1)} all-reduce(f32[64]{0:T(128)S(1)} %copy-done.1), channel_id=1, replica_groups=mesh['row'=8,'col'=4] {'row'}, use_global_device_ids=true, to_apply=%region_11.12 | all-reduce | flops 64 | bytes 512 | tf_op jit(solution)/shard_map/psum | solution.py:70
  368.2 4.6 %all-reduce.14.cloned.1.call-done = f32[64,6144]{1,0:T(8,128)} async-done(((f32[64,6144]{1,0:T(8,128)}), f32[64,6144]{1,0:T(8,128)}) %all-reduce.14.cloned.1.call-update) | async-done | bytes 1572880 | tf_op jit(solution)/shard_map/psum | solution.py:52
  372.8 4.0 %multiply_subtract_fusion = (f32[64,6144]{1,0:T(8,128)}, f32[64,6144]{1,0:T(8,128)}) fusion(f32[64,6144]{1,0:T(8,128)S(1)} %multiply_subtract_fusion.1, f32[64,6144]{1,0:T(8,128)} %all-reduce.14.cloned.1.call-done, f32[64,6144]{1,0:T(8,128)} %get-tuple-element.3, f32[64]{0:T(128)S(1)} %add_divide_fusion, f32[64,6144]{1,0:T(8,128)S(1)} %copy-done, ...), kind=kLoop, calls=%fused_computation.12 | loop fusion | flops 2752512 | bytes 9437696 | tf_op jit(solution)/shard_map/sub | solution.py:75
  (35 shorter events, 12.5 us)
Async XLA Ops:
  7.2 72.5 %all-reduce.6.cloned.1.call-start = ((), (), s32[]{:S(2)}) async-start(), calls=%async_computation | async-start | bytes 3145728 | tf_op jit(solution)/shard_map/psum | solution.py:52
  17.9 115.0 %all-reduce.8.cloned.1.call-start = ((), (), s32[]{:S(2)}) async-start(), calls=%async_computation.1 | async-start | bytes 1572864 | tf_op jit(solution)/shard_map/psum | solution.py:69
  89.7 111.7 %all-reduce.10.cloned.1.call-start = ((), (), s32[]{:S(2)}) async-start(), calls=%async_computation.2 | async-start | bytes 3145728 | tf_op jit(solution)/shard_map/psum | solution.py:52
  142.4 1.4 copy-start
  142.4 158.4 %all-reduce.12.cloned.1.call-start = ((), (), s32[]{:S(2)}) async-start(), calls=%async_computation.3 | async-start | bytes 1572864 | tf_op jit(solution)/shard_map/psum | solution.py:69
  242.8 1.7 copy-start.2
  257.2 115.6 %all-reduce.14.cloned.1.call-start = ((), (), s32[]{:S(2)}) async-start(), calls=%async_computation.4 | async-start | bytes 3145728 | tf_op jit(solution)/shard_map/psum | solution.py:52
  314.2 41.0 %copy-start.1 = (f32[64]{0:T(128)S(1)}, f32[64]{0:T(128)}, u32[]{:S(2)}) copy-start(f32[64]{0:T(128)} %get-tuple-element.7) | copy-start | bytes 772
  314.2 54.0 %copy-start.3 = (f32[64]{0:T(128)S(1)}, f32[64]{0:T(128)}, u32[]{:S(2)}) copy-start(f32[64]{0:T(128)} %copy-done.2) | copy-start | bytes 772
Sparse Core Ops, SparseCore 0:
  18.0 61.6 all-reduce.5
  89.8 43.0 all-reduce.7
  142.6 58.7 all-reduce.9
  257.3 43.4 all-reduce.11
  314.4 58.3 all-reduce.13
where the time goes:
time: 384 us; the launch traced here: 383 us
  waiting for transfers between devices  158 us (41%)
  blocking collectives  145 us (38%)
  matrix products  33.8 us (9%)
  other arithmetic  16.4 us (4%)
  local copies, waits for them, and re-layouts  15.9 us (4%)
  between operations  13.9 us (4%)
    psum x2, waiting for transfers between devices, per_device(): forward_image = lax.psum(forward_partial_value, 'col')  86.7 us
    psum x3, waiting for transfers between devices, backward(): return lax.psum(partial_value, 'row')  71 us
    psum x1, blocking collectives, per_device(): dir_norm = lax.psum(frame_product(direction, direction), ('row', 'col'))  40 us
    psum x1, blocking collectives, per_device(): norm_now = lax.psum(frame_product(residual, residual), ('row', 'col'))  39.8 us
    psum x1, blocking collectives, per_device(): norm_next = lax.psum(frame_product(residual, residual), ('row', 'col'))  39.7 us
    psum x2, blocking collectives, per_device(): image_norm = lax.psum(jnp.sum(forward_image * forward_image, axis=1), 'row')  25.8 us
    dot_general x3, matrix products, padded_apply(): jnp.einsum('fijr,ijmr->fjm', scaled, second_factor, preferred_element_typ...  19.5 us
    dot_general x2, matrix products, padded_apply(): jnp.einsum('fijr,ijsr->fis', scaled, second_factor, preferred_element_typ...  14.3 us
  transfers between devices with their start and end apart: 5, of which 5 were waited for; matrix products, arithmetic and copies ran while one was open for 0% of the time, Pallas kernels for 0%

commit v1 on v0

--- a/solution.py
+++ b/solution.py
@@ -74,7 +74,7 @@
         solution_field = solution_field + step_size[:, None] * direction
         residual = residual - step_size[:, None] * operator_image
         if sweep + 1 < ITERS:
-            norm_next = lax.psum(frame_product(residual, residual), ("row", "col"))
+            norm_next = lax.psum(lax.psum(frame_product(residual, residual), "col"), "row")
             growth = norm_next / (norm_now + epsilon)
             direction = residual + growth[:, None] * direction
             norm_now = norm_next

time: 384 us -> 364 us (0.948)
  blocking collectives: 145 us -> 129 us
  waiting for transfers between devices: 158 us -> 154 us
    psum x1 -> x2, blocking collectives: 39.7 us -> 23.7 us  [the longest x1 12 us: per_device(): lax.psum(lax.psum(frame_product(residual, residual), 'col'), 'row')]
where the time goes in v1:
time: 364 us
  waiting for transfers between devices  154 us (42%)
  blocking collectives  129 us (35%)
  matrix products  33.8 us (9%)
  other arithmetic  16.4 us (5%)
  local copies, waits for them, and re-layouts  15.8 us (4%)
  between operations  13.9 us (4%)
    psum x2, waiting for transfers between devices, per_device(): forward_image = lax.psum(forward_partial_value, 'col')  83.1 us
    psum x3, waiting for transfers between devices, backward(): return lax.psum(partial_value, 'row')  71.1 us
    psum x1, blocking collectives, per_device(): dir_norm = lax.psum(frame_product(direction, direction), ('row', 'col'))  39.9 us
    psum x1, blocking collectives, per_device(): norm_now = lax.psum(frame_product(residual, residual), ('row', 'col'))  39.8 us
    psum x2, blocking collectives, per_device(): image_norm = lax.psum(jnp.sum(forward_image * forward_image, axis=1), 'row')  25.8 us
    dot_general x3, matrix products, padded_apply(): jnp.einsum('fijr,ijmr->fjm', scaled, second_factor, preferred_element_typ...  19.5 us
    dot_general x2, matrix products, padded_apply(): jnp.einsum('fijr,ijsr->fis', scaled, second_factor, preferred_element_typ...  14.3 us
    psum x1, blocking collectives, per_device(): lax.psum(lax.psum(frame_product(residual, residual), 'col'), 'row')  12 us
  transfers between devices with their start and end apart: 5, of which 5 were waited for; matrix products, arithmetic and copies ran while one was open for 0% of the time, Pallas kernels for 0%

profile of v1, /device:TPU:0, one launch (start us, length us, event | category | flops | bytes accessed | tf_op | source)
XLA Modules:
  0.0 363.7 jit_solution(5612224546363961218)
XLA Ops:
  10.4 6.1 %fusion.12 = f32[6,8,8,1024]{3,2,1,0:T(8,128)S(1)} fusion(bf16[3,6,1024,128]{3,2,1,0:T(8,128)(2,1)} %param.6, bf16[3,6,1024,128]{3,2,1,0:T(8,128)(2,1)} %param.5, bf16[64,3,1024,1]{2,1,0,3:T(4,128)(2,1)S(1)} %reshape.49, f32[3,6,128]{2,0,1:T(4,128)S(1)} %copy.12), kind=kOutput, calls=%fused_computation.16 | convolution fusion | flops 604274688 | bytes 11412480 | tf_op jit(solution)/shard_map/fijr,ijmr->fjm/dot_general | solution.py:27
  17.8 61.8 %all-reduce.6.cloned.1.call-done = f32[64,6144]{1,0:T(8,128)} async-done(((f32[64,6144]{1,0:T(8,128)}), f32[64,6144]{1,0:T(8,128)}) %all-reduce.6.cloned.1.call-update) | async-done | bytes 1572880 | tf_op jit(solution)/shard_map/psum | solution.py:52
  82.1 6.6 %convolution_bitcast_fusion.1 = f32[3,8,8,1024]{3,2,1,0:T(8,128)S(1)} fusion(bf16[3,6,1024,128]{3,2,1,0:T(8,128)(2,1)} %param.5, bf16[3,6,1024,128]{3,2,1,0:T(8,128)(2,1)} %param.6, bf16[64,6,1024,1]{2,1,0,3:T(8,128)(2,1)S(1)} %reshape.51, f32[3,6,128]{2,1,0:T(8,128)S(1)} %fusion.73), kind=kOutput, calls=%fused_computation.20 | convolution fusion | flops 604274688 | bytes 11019264 | tf_op jit(solution)/shard_map/fijr,ijsr->fis/dot_general | solution.py:36
  89.7 43.1 %all-reduce.8.cloned.1.call-done = f32[64,3072]{1,0:T(8,128)} async-done(((f32[64,3072]{1,0:T(8,128)}), f32[64,3072]{1,0:T(8,128)}) %all-reduce.8.cloned.1.call-update) | async-done | bytes 786448 | tf_op jit(solution)/shard_map/psum | solution.py:69
  132.8 1.6 multiply_reduce_fusion.1
  134.9 6.1 %fusion.15 = f32[6,8,8,1024]{3,2,1,0:T(8,128)S(1)} fusion(bf16[3,6,1024,128]{3,2,1,0:T(8,128)(2,1)} %param.6, bf16[3,6,1024,128]{3,2,1,0:T(8,128)(2,1)} %param.5, bf16[64,3,1024,1]{2,1,0,3:T(4,128)(2,1)S(1)} %reshape.53, f32[3,6,128]{2,0,1:T(4,128)S(1)} %copy.12), kind=kOutput, calls=%fused_computation.17 | convolution fusion | flops 604274688 | bytes 11412480 | tf_op jit(solution)/shard_map/fijr,ijmr->fjm/dot_general | solution.py:27
  143.8 39.8 %psum.81 = f32[64]{0:T(128)S(1)} all-reduce(f32[64]{0:T(128)S(1)} %multiply_reduce_fusion.4), channel_id=1, replica_groups=mesh['row'=8,'col'=4] {'row','col'}, use_global_device_ids=true, to_apply=%region_2.3 | all-reduce | flops 64 | bytes 512 | tf_op jit(solution)/shard_map/psum | solution.py:64
  183.6 12.9 %psum.83 = f32[64]{0:T(128)S(1)} all-reduce(f32[64]{0:T(128)S(1)} %get-tuple-element.8), channel_id=1, replica_groups=mesh['row'=8,'col'=4] {'row'}, use_global_device_ids=true, to_apply=%region_5.6 | all-reduce | flops 64 | bytes 512 | tf_op jit(solution)/shard_map/psum | solution.py:70
  196.5 4.7 %all-reduce.10.cloned.1.call-done = f32[64,6144]{1,0:T(8,128)} async-done(((f32[64,6144]{1,0:T(8,128)}), f32[64,6144]{1,0:T(8,128)}) %all-reduce.10.cloned.1.call-update) | async-done | bytes 1572880 | tf_op jit(solution)/shard_map/psum | solution.py:52
  201.2 1.7 multiply_subtract_fusion.1
  203.0 11.8 %psum.85 = f32[64]{0:T(128)S(1)} all-reduce(f32[64]{0:T(128)S(1)} %multiply_reduce_fusion.3), channel_id=1, replica_groups=mesh['row'=8,'col'=4] {'col'}, use_global_device_ids=true, to_apply=%region_8.9 | all-reduce | flops 64 | bytes 512 | tf_op jit(solution)/shard_map/psum | solution.py:77
  214.8 12.0 %psum.86 = f32[64]{0:T(128)S(1)} all-reduce(f32[64]{0:T(128)S(1)} %psum.85), channel_id=1, replica_groups=mesh['row'=8,'col'=4] {'row'}, use_global_device_ids=true, to_apply=%region_9.10 | all-reduce | flops 64 | bytes 512 | tf_op jit(solution)/shard_map/psum | solution.py:77
  226.8 1.7 fusion.74
  228.5 2.8 reshape.55
  231.3 7.7 %convolution_bitcast_fusion = f32[3,8,8,1024]{3,2,1,0:T(8,128)} fusion(bf16[3,6,1024,128]{3,2,1,0:T(8,128)(2,1)} %param.5, bf16[3,6,1024,128]{3,2,1,0:T(8,128)(2,1)} %param.6, bf16[64,6,1024,1]{2,1,0,3:T(8,128)(2,1)} %reshape.55, f32[3,6,128]{2,1,0:T(8,128)S(1)} %fusion.73), kind=kOutput, calls=%fused_computation.19 | convolution fusion | flops 604274688 | bytes 11019264 | tf_op jit(solution)/shard_map/fijr,ijsr->fis/dot_general | solution.py:36
  239.0 2.1 copy.36
  241.2 40.0 %all-reduce.12.cloned.1.call-done = f32[64,3072]{1,0:T(8,128)} async-done(((f32[64,3072]{1,0:T(8,128)}), f32[64,3072]{1,0:T(8,128)}) %all-reduce.12.cloned.1.call-update) | async-done | bytes 786448 | tf_op jit(solution)/shard_map/psum | solution.py:69
  281.2 2.1 fusion.75
  284.5 7.4 %fusion.18 = f32[6,8,8,1024]{3,2,1,0:T(8,128)} fusion(bf16[3,6,1024,128]{3,2,1,0:T(8,128)(2,1)} %param.6, bf16[3,6,1024,128]{3,2,1,0:T(8,128)(2,1)} %param.5, bf16[64,3,1024,1]{2,1,0,3:T(4,128)(2,1)} %reshape.57, f32[3,6,128]{2,0,1:T(4,128)S(1)} %copy.12), kind=kOutput, calls=%fused_computation.18 | convolution fusion | flops 604274688 | bytes 11412480 | tf_op jit(solution)/shard_map/fijr,ijmr->fjm/dot_general | solution.py:27
  291.9 2.7 copy.37
  295.7 39.9 %psum.89 = f32[64]{0:T(128)S(1)} all-reduce(f32[64]{0:T(128)S(1)} %multiply_reduce_fusion.2), channel_id=1, replica_groups=mesh['row'=8,'col'=4] {'row','col'}, use_global_device_ids=true, to_apply=%region_14.15 | all-reduce | flops 64 | bytes 512 | tf_op jit(solution)/shard_map/psum | solution.py:71
  335.6 12.9 %psum.88 = f32[64]{0:T(128)S(1)} all-reduce(f32[64]{0:T(128)S(1)} %copy-done.1), channel_id=1, replica_groups=mesh['row'=8,'col'=4] {'row'}, use_global_device_ids=true, to_apply=%region_12.13 | all-reduce | flops 64 | bytes 512 | tf_op jit(solution)/shard_map/psum | solution.py:70
  348.6 4.6 %all-reduce.14.cloned.1.call-done = f32[64,6144]{1,0:T(8,128)} async-done(((f32[64,6144]{1,0:T(8,128)}), f32[64,6144]{1,0:T(8,128)}) %all-reduce.14.cloned.1.call-update) | async-done | bytes 1572880 | tf_op jit(solution)/shard_map/psum | solution.py:52
  353.2 4.0 %multiply_subtract_fusion = (f32[64,6144]{1,0:T(8,128)}, f32[64,6144]{1,0:T(8,128)}) fusion(f32[64,6144]{1,0:T(8,128)S(1)} %multiply_subtract_fusion.1, f32[64,6144]{1,0:T(8,128)} %all-reduce.14.cloned.1.call-done, f32[64,6144]{1,0:T(8,128)} %get-tuple-element.3, f32[64]{0:T(128)S(1)} %add_divide_fusion, f32[64,6144]{1,0:T(8,128)S(1)} %copy-done, ...), kind=kLoop, calls=%fused_computation.12 | loop fusion | flops 2752512 | bytes 9437696 | tf_op jit(solution)/shard_map/sub | solution.py:75
  (36 shorter events, 13.9 us)
Async XLA Ops:
  7.2 72.4 %all-reduce.6.cloned.1.call-start = ((), (), s32[]{:S(2)}) async-start(), calls=%async_computation | async-start | bytes 3145728 | tf_op jit(solution)/shard_map/psum | solution.py:52
  17.8 115.0 %all-reduce.8.cloned.1.call-start = ((), (), s32[]{:S(2)}) async-start(), calls=%async_computation.1 | async-start | bytes 1572864 | tf_op jit(solution)/shard_map/psum | solution.py:69
  89.6 111.6 %all-reduce.10.cloned.1.call-start = ((), (), s32[]{:S(2)}) async-start(), calls=%async_computation.2 | async-start | bytes 3145728 | tf_op jit(solution)/shard_map/psum | solution.py:52
  142.3 1.4 copy-start
  142.3 138.9 %all-reduce.12.cloned.1.call-start = ((), (), s32[]{:S(2)}) async-start(), calls=%async_computation.3 | async-start | bytes 1572864 | tf_op jit(solution)/shard_map/psum | solution.py:69
  226.8 1.7 copy-start.2
  241.1 112.1 %all-reduce.14.cloned.1.call-start = ((), (), s32[]{:S(2)}) async-start(), calls=%async_computation.4 | async-start | bytes 3145728 | tf_op jit(solution)/shard_map/psum | solution.py:52
  294.6 41.0 %copy-start.1 = (f32[64]{0:T(128)S(1)}, f32[64]{0:T(128)}, u32[]{:S(2)}) copy-start(f32[64]{0:T(128)} %get-tuple-element.7) | copy-start | bytes 772
  294.6 54.0 %copy-start.3 = (f32[64]{0:T(128)S(1)}, f32[64]{0:T(128)}, u32[]{:S(2)}) copy-start(f32[64]{0:T(128)} %copy-done.2) | copy-start | bytes 772
Sparse Core Ops, SparseCore 0:
  17.9 61.6 all-reduce.5
  89.7 43.0 all-reduce.7
  142.4 58.7 all-reduce.9
  241.2 39.8 all-reduce.11
  294.8 58.3 all-reduce.13
